TPU v7x, 32 devices: a whole 2x2x4 slice. The times are simulated.
32 devices in a mesh: row: 4 (over z), col: 8 (over y, x, core).
Axes of the slice: x: 2, y: 2, z: 4, core: 2. Of those that a mesh axis runs over, the one named last changes fastest.
Arguments:
- field: float32 [32, 196608], P(None, ('row', 'col')), may hold values from -6 to 6
- incident: float32 [32, 98304], P(None, 'col'), may hold values from -6 to 6
- elem_mat: float32 [4, 4, 1179648], P(None, None, ('row', 'col')), may hold values from -1.5 to 1.5
- connect: int32 [4, 1179648], P(None, ('row', 'col')), may hold values from 0 to 9215
- halo_lists: int32 [32, 2, 1536], P(('row', 'col')), may hold values from 0 to 6143
- bem_rows: float32 [256, 98304], P('row', 'col'), may hold values from -0.01953125 to 0.01953125
- send_node: int32 [32, 8, 768], P(('row', 'col')), may hold values from 0 to 6143, as said below
- send_count: int32 [32, 8], P(('row', 'col')), may hold values from 0 to 768, as said below
- block_slots: int32 [8, 32, 768], P('col'), may hold values from 0 to 12287, as said below
Outputs:
- fem_out: float32 [32, 196608], P(None, ('row', 'col'))
- bem_out: float32 [32, 256], P(None, 'row')
Inputs may be any that keep to these rules, and one draw needn't show every extreme that they name: `send_count`: each column block's 12288 positions are split among the partitions' live slots; in every block some partition fills all 768 slots. `send_node`: live slots of one partition name distinct own nodes; slots at or beyond the count hold 0. `block_slots`: the live slots of all partitions cover each position of block c exactly once; slots at or beyond the count hold 0.
All inputs are finite; a program needn't handle non-finite values.
Results may differ from a plain program's by a relative error of at most 0.0003.
Values sent between devices are 32-bit elements; how exact they have to be, the bound alone decides.
A program may use at most 256 MiB of HBM per device.

v0:
```python
import jax
import jax.numpy as jnp
from jax import lax
from jax.sharding import PartitionSpec as P

S = 32


def padded_2(block, sides, width):
    for axis, dim in sides:
        count = lax.axis_size(axis)
        forward = [(i, i + 1) for i in range(count - 1)]
        backward = [(target, source) for source, target in forward]
        low = lax.ppermute(
            lax.slice_in_dim(block, block.shape[dim] - width, None, axis=dim), axis, forward
        )
        high = lax.ppermute(lax.slice_in_dim(block, 0, width, axis=dim), axis, backward)
        block = jnp.concatenate([low, block, high], axis=dim)
    return block


def element_apply(extended, conn, mats, node_count, halo):
    gathered = extended[:, conn]
    terms = []
    for a in range(4):
        accum = mats[a, 0][None, :] * gathered[:, 0]
        for b in range(1, 4):
            accum = accum + mats[a, b][None, :] * gathered[:, b]
        terms.append(accum)
    element_terms = jnp.stack(terms, axis=1)
    owned_rows = conn - halo
    inside = (owned_rows >= 0) & (owned_rows < node_count)
    target = jnp.where(inside, owned_rows, node_count)
    result = jnp.zeros((extended.shape[0], node_count), jnp.float32)
    return result.at[:, target.reshape(-1)].add(
        element_terms.reshape(extended.shape[0], -1), mode="drop"
    )


def shards(
    field, incident, elem_mat, connect, halo_lists, bem_rows, send_node, send_count, block_slots
):
    node_count = field.shape[1]
    halo = halo_lists.shape[2]
    blocks = send_node.shape[1]
    slot_cap = send_node.shape[2]
    picked = field[:, send_node[0].reshape(-1)].reshape(S, blocks, slot_cap)
    live_slots = jnp.arange(slot_cap, dtype=jnp.int32)[None, :] < send_count[0][:, None]
    picked = jnp.where(live_slots[None], picked, jnp.zeros_like(picked))
    outgoing = jnp.transpose(picked, (1, 0, 2))
    copies = lax.axis_size("row")
    spread = jnp.broadcast_to(outgoing[None], (copies,) + outgoing.shape).reshape(
        (copies * blocks,) + outgoing.shape[1:]
    )
    arrived = lax.all_to_all(spread, ("row", "col"), split_axis=0, concat_axis=0, tiled=True)
    values = jnp.transpose(arrived, (1, 0, 2)).reshape(S, -1)
    surface = incident.at[:, block_slots[0].reshape(-1)].add(values)
    outbound = field[:, halo_lists[0].reshape(-1)]
    padded = padded_2(outbound, ((("row", "col"), 1),), halo)
    extended = jnp.concatenate([padded[:, :halo], field, padded[:, 3 * halo :]], axis=1)
    fem_out = element_apply(extended, connect, elem_mat, node_count, halo)
    partial_rows = lax.dot_general(
        surface,
        bem_rows,
        (((1,), (1,)), ((), ())),
        precision=lax.Precision.HIGHEST,
        preferred_element_type=jnp.float32,
    )
    bem_out = lax.psum(partial_rows, "col")
    return (fem_out, bem_out)


def solution(mesh):
    return jax.shard_map(
        shards,
        mesh=mesh,
        in_specs=(
            P(None, ("row", "col")),
            P(None, "col"),
            P(None, None, ("row", "col")),
            P(None, ("row", "col")),
            P(("row", "col"), None, None),
            P("row", "col"),
            P(("row", "col"), None, None),
            P(("row", "col"), None),
            P("col", None, None),
        ),
        out_specs=(P(None, ("row", "col")), P(None, "row")),
        check_vma=False,
    )
```

profile of v0, /device:TPU:16, one launch (start us, length us, event | category | flops | bytes accessed | tf_op | source)
XLA Modules:
  0.0 1729.9 jit_solution(11953365362754512024)
XLA Ops:
  1.6 3.2 copy.25
  4.7 12.8 gather_fusion
  17.5 2.7 fusion.4
  20.2 2.1 copy.27
  22.2 3.7 collective-permute-start.1
  25.9 2.1 copy.26
  28.0 1.9 collective-permute-start
  30.1 23.0 %gather_fusion.2 = f32[6144,32]{1,0:T(8,128)} fusion(f32[32,6144]{0,1:T(8,128)} %copy.25, s32[6144]{0:T(1024)S(1)} %broadcast_clamp_fusion.1), kind=kCustom, calls=%fused_computation.2 | custom fusion | bytes 1597440 | tf_op jit(solution)/shard_map/gather | solution.py:47
  53.0 4.7 select_bitcast_fusion
  57.7 3.1 copy.33
  60.8 3.2 broadcast_in_dim.35
  64.0 6.2 all-to-all-start
  71.0 1.4 fusion.2
  74.5 2.9 fusion.3
  78.2 5.0 copy.35
  83.2 2.4 pad_maximum_fusion
  85.6 3.9 copy.28
  89.5 536.7 %gather_fusion.1 = f32[147456,32]{1,0:T(8,128)} fusion(f32[32,9216]{0,1:T(8,128)} %copy.28, s32[147456]{0:T(1024)} %broadcast_clamp_fusion), kind=kCustom, calls=%fused_computation.1 | custom fusion | bytes 38338560 | tf_op jit(solution)/shard_map/gather | solution.py:23
  626.2 45.4 %copy.29 = f32[4,36864,32]{1,2,0:T(8,128)} copy(f32[4,36864,32]{2,1,0:T(8,128)} %bitcast.4) | data formatting | bytes 37748736 | tf_op jit(solution)/shard_map/gather | solution.py:23
  671.6 12.0 multiply_add_fusion.1
  683.6 3.5 copy-done.1
  687.2 5.9 multiply_add_fusion.3
  693.0 7.6 maximum_bitcast_fusion
  700.7 6.8 copy.38
  707.4 39.2 %copy.31 = f32[147456,32]{1,0:T(8,128)} copy(f32[147456,32]{0,1:T(8,128)} %bitcast.61) | data formatting | bytes 37748736 | tf_op jit(solution)/shard_map/reshape | solution.py:36
  746.6 782.2 %scatter_custom_fusion = f32[32,6144]{0,1:T(8,128)} fusion(s32[147456]{0:T(1024)} %bitcast.84, f32[147456,32]{1,0:T(8,128)} %copy.31, f32[]{:T(128)} %constant.6.clone.1), kind=kCustom, calls=%fused_computation.13 | custom fusion | flops 4718592 | bytes 786944 | tf_op jit(solution)/shard_map/scatter-add | solution.py:35
  1528.8 3.1 copy.37
  1531.9 3.8 copy.39
  1535.7 8.4 copy.36
  1544.1 149.0 %scatter_fusion = f32[32,12288]{0,1:T(8,128)} fusion(f32[32,12288]{0,1:T(8,128)} %copy.35, s32[24576]{0:T(1024)S(1)} %bitcast.86, f32[24576,32]{1,0:T(8,128)} %copy.36), kind=kCustom, calls=%fused_computation.4 | custom fusion | flops 786432 | bytes 9535488 | tf_op jit(solution)/shard_map/scatter-add | solution.py:57
  1693.1 11.9 fusion.5
  1705.0 24.9 %psum.7 = f32[32,64]{1,0:T(8,128)} all-reduce(f32[32,64]{1,0:T(8,128)S(1)} %fusion.5), channel_id=1, replica_groups=mesh['row'=4,'col'=8] {'col'}, use_global_device_ids=true, to_apply=%region_2.3 | all-reduce | flops 2048 | bytes 16384 | tf_op jit(solution)/shard_map/psum | solution.py:69
  (31 shorter events, 4.8 us)
Async XLA Ops:
  0.6 1692.5 %copy-start = (f32[64,12288]{1,0:T(8,128)S(1)}, f32[64,12288]{1,0:T(8,128)}, u32[]{:S(2)}) copy-start(f32[64,12288]{1,0:T(8,128)} %param.14) | copy-start | bytes 9437188
  4.7 25.2 %copy-start.7 = (s32[1,8]{1,0:T(1,128)S(1)}, s32[1,8]{1,0:T(1,128)}, u32[]{:S(2)}) copy-start(s32[1,8]{1,0:T(1,128)} %param.16) | copy-start | bytes 100
  4.7 25.3 %copy-start.6 = (s32[1,8,768]{2,1,0:T(8,128)S(1)}, s32[1,8,768]{2,1,0:T(8,128)}, u32[]{:S(2)}) copy-start(s32[1,8,768]{2,1,0:T(8,128)} %param.15) | copy-start | bytes 73732
  22.2 61.0 %collective-permute-start.1 = (f32[32,1536]{1,0:T(8,128)}, f32[32,1536]{1,0:T(8,128)}, u32[]{:S(2)}, u32[]{:S(2)}) collective-permute-start(f32[32,1536]{1,0:T(8,128)} %copy.27), channel_id=1, source_target_pairs={{1,0},{2,1},{3,2},{4,3},{5,4},{6,5},{7,6},{8,7},{9,8},{10,9},{11,1... | collective-permute-start | bytes 589832 | tf_op jit(solution)/shard_map/ppermute | solution.py:17
  28.0 55.2 %collective-permute-start = (f32[32,1536]{1,0:T(8,128)}, f32[32,1536]{1,0:T(8,128)}, u32[]{:S(2)}, u32[]{:S(2)}) collective-permute-start(f32[32,1536]{1,0:T(8,128)} %copy.26), channel_id=1, source_target_pairs={{0,1},{1,2},{2,3},{3,4},{4,5},{5,6},{6,7},{7,8},{8,9},{9,10},{10,1... | collective-permute-start | bytes 589832 | tf_op jit(solution)/shard_map/ppermute | solution.py:14
  60.8 9.4 copy-start.5
  64.0 1467.9 %all-to-all-start = ((f32[32,32,768]{2,1,0:T(8,128)}), f32[32,32,768]{2,1,0:T(8,128)}, u32[]{:S(2)}, u32[]{:S(2)}) async-start(f32[32,32,768]{2,1,0:T(8,128)} %bitcast.62), calls=%async_computation | async-start | bytes 6291456 | tf_op jit(solution)/shard_map/all_to_all | solution.py:55
  70.1 4.3 copy-start.2
  671.6 15.6 copy-start.1
  671.6 15.6 copy-start.3
  1535.7 8.4 copy-start.4
where the time goes:
time: 1740 us; the launch traced here: 1730 us
  other arithmetic  968 us (56%)
  local copies, waits for them, and re-layouts  712 us (41%)
  blocking collectives  24.9 us (1%)
    scatter-add x1, other arithmetic, element_apply(): result.at[:, target.reshape(-1)]  782 us
    gather x2, local copies, waits for them, and re-layouts, element_apply(): gathered = extended[:, conn]  582 us
    scatter-add x1, other arithmetic, shards(): surface = incident.at[:, block_slots[0].reshape(-1)].add(values)  149 us
    reshape x2, local copies, waits for them, and re-layouts, element_apply(): element_terms.reshape(extended.shape[0], -1)  46 us
  transfers between devices with their start and end apart: 3, of which 0 were waited for; matrix products, arithmetic and copies ran while one was open for 86% of the time, Pallas kernels for 0%

commit v1 on v0

v1 whole, which is shorter than its diff:
```python
import functools

import jax
import jax.numpy as jnp
from jax import lax
from jax.experimental import pallas as pl
from jax.experimental.pallas import tpu as pltpu
from jax.sharding import PartitionSpec as P

S = 32
LANES = 128
GROUP = 4 * LANES
SETS = 2
UNROLL = 64
VMEM_BYTES = 60 * 2**20


def lane_iota():
    return lax.broadcasted_iota(jnp.int32, (1, LANES), 1)


def quarter(parts):
    lane = lane_iota()
    low = jnp.where(lane < S, parts[0], parts[1])
    high = jnp.where(lane < 3 * S, parts[2], parts[3])
    return jnp.where(lane < 2 * S, low, high)


def aligned(start, size=LANES):
    return pl.ds(pl.multiple_of(start, LANES), size)


def fill_table(table, first, source):
    def step(i, carry):
        block = source[:, aligned(i * LANES)]
        table[aligned(first + i * LANES), :] = jnp.concatenate([block] * 4, axis=0).T
        return carry

    lax.fori_loop(0, source.shape[1] // LANES, step, 0)


def gather_rows(table, index, base, rows):
    def step(j, carry):
        start = pl.multiple_of(j * UNROLL, UNROLL)
        for u in range(UNROLL):
            picked = [
                table[pl.ds(index[base + b * LANES + start + u], 1), :] for b in range(4)
            ]
            rows[pl.ds(start + u, 1), :] = quarter(picked)
        return carry

    lax.fori_loop(0, LANES // UNROLL, step, 0)


def pick_kernel(index, field, out, table, rows):
    fill_table(table, 0, field)

    def group(k, carry):
        gather_rows(table, index, k * GROUP, rows)
        turned = rows[...].T
        for b in range(4):
            out[:, aligned(k * GROUP + b * LANES)] = turned[S * b : S * b + S]
        return carry

    lax.fori_loop(0, out.shape[1] // GROUP, group, 0)


def pick(index, field):
    return pl.pallas_call(
        pick_kernel,
        in_specs=[
            pl.BlockSpec(memory_space=pltpu.SMEM),
            pl.BlockSpec(memory_space=pltpu.VMEM),
        ],
        out_specs=pl.BlockSpec(memory_space=pltpu.VMEM),
        out_shape=jax.ShapeDtypeStruct((S, index.shape[0]), jnp.float32),
        scratch_shapes=[
            pltpu.VMEM((field.shape[1], LANES), jnp.float32),
            pltpu.VMEM((LANES, LANES), jnp.float32),
        ],
        compiler_params=pltpu.CompilerParams(vmem_limit_bytes=VMEM_BYTES),
        name="pick",
    )(index, field)


def element_kernel(halo, index, mats, low, field, high, out, table, rows, terms, *sums):
    step = pl.program_id(0)
    nodes = field.shape[1]

    @pl.when(step == 0)
    def _():
        fill_table(table, 0, low)
        fill_table(table, halo, field)
        fill_table(table, halo + nodes, high)

        def clear(i, carry):
            for total in sums:
                total[aligned(i * LANES), :] = jnp.zeros((LANES, LANES), jnp.float32)
            return carry

        lax.fori_loop(0, table.shape[0] // LANES, clear, 0)

    def block(k, carry):
        base = k * GROUP
        gather_rows(table, index, base, rows)
        turned = rows[...].T
        here = aligned(k * LANES)
        parts = []
        for a in range(4):
            part = mats[a, 0:1, here] * turned[0:S]
            for b in range(1, 4):
                part = part + mats[a, b : b + 1, here] * turned[S * b : S * b + S]
            parts.append(part)
        terms[...] = jnp.concatenate(parts, axis=0).T

        def scatter(j, inner):
            start = pl.multiple_of(j * UNROLL, UNROLL)
            for u in range(0, UNROLL, SETS):
                places, values = [], []
                for p in range(SETS):
                    term = terms[pl.ds(start + u + p, 1), :]
                    for a in range(4):
                        place = pl.ds(index[base + a * LANES + start + u + p], 1)
                        places.append(place)
                        values.append(sums[4 * p + a][place, :] + term)
                for total, place, value in zip(sums, places, values):
                    total[place, :] = value
            return inner

        lax.fori_loop(0, LANES // UNROLL, scatter, 0)
        return carry

    lax.fori_loop(0, mats.shape[2] // LANES, block, 0)

    @pl.when(step == pl.num_programs(0) - 1)
    def _():
        def finish(i, carry):
            here = aligned(i * LANES + halo)
            added = [
                sum(sums[4 * p + a][here, :] for p in range(1, SETS)) + sums[a][here, :]
                for a in range(4)
            ]
            turned = quarter(added).T
            out[:, aligned(i * LANES)] = (
                turned[0:S] + turned[S : 2 * S] + turned[2 * S : 3 * S] + turned[3 * S :]
            )
            return carry

        lax.fori_loop(0, nodes // LANES, finish, 0)


def element_apply(index, mats, low, field, high):
    halo, nodes = low.shape[1], field.shape[1]
    elements = mats.shape[2]
    blocks = next(n for n in (16, 12, 8, 4, 2) if elements % (n * LANES) == 0)
    table = pltpu.VMEM((nodes + 2 * halo, LANES), jnp.float32)
    square = pltpu.VMEM((LANES, LANES), jnp.float32)
    whole = pl.BlockSpec(memory_space=pltpu.VMEM)
    return pl.pallas_call(
        functools.partial(element_kernel, halo),
        grid=(elements // (blocks * LANES),),
        in_specs=[
            pl.BlockSpec((blocks * GROUP,), lambda i: (i,), memory_space=pltpu.SMEM),
            pl.BlockSpec((4, 4, blocks * LANES), lambda i: (0, 0, i)),
            whole,
            whole,
            whole,
        ],
        out_specs=whole,
        out_shape=jax.ShapeDtypeStruct((S, nodes), jnp.float32),
        scratch_shapes=[table, square, square] + [table] * (4 * SETS),
        compiler_params=pltpu.CompilerParams(vmem_limit_bytes=VMEM_BYTES),
        name="elements",
    )(index, mats, low, field, high)


def surface_kernel(index, values, incident, bem, out, surface, *rows):
    lane = lane_iota()

    def group(k, carry):
        stacked = jnp.concatenate(
            [values[:, aligned(k * GROUP + q * LANES)] for q in range(4)], axis=0
        )
        turned = stacked.T
        for q in range(4):
            rows[q][...] = jnp.where(
                (lane >= S * q) & (lane < S * q + S), turned, jnp.zeros_like(turned)
            )

        def scatter(j, inner):
            start = pl.multiple_of(j * UNROLL, UNROLL)
            for u in range(UNROLL):
                for q in range(4):
                    place = index[k * GROUP + q * LANES + start + u]
                    surface[pl.ds(place, 1), :] = rows[q][pl.ds(start + u, 1), :]
            return inner

        lax.fori_loop(0, LANES // UNROLL, scatter, 0)
        return carry

    lax.fori_loop(0, values.shape[1] // GROUP, group, 0)
    surface[0:1, :] = jnp.zeros((1, LANES), jnp.float32)
    spread = jnp.dot(
        bem[...],
        surface[...],
        precision=lax.Precision.HIGHEST,
        preferred_element_type=jnp.float32,
    ).T
    direct = lax.dot_general(
        incident[...],
        bem[...],
        (((1,), (1,)), ((), ())),
        precision=lax.Precision.HIGHEST,
        preferred_element_type=jnp.float32,
    )
    out[...] = (
        direct + spread[0:S] + spread[S : 2 * S] + spread[2 * S : 3 * S] + spread[3 * S :]
    )


def surface_apply(index, values, incident, bem):
    whole = pl.BlockSpec(memory_space=pltpu.VMEM)
    square = pltpu.VMEM((LANES, LANES), jnp.float32)
    return pl.pallas_call(
        surface_kernel,
        in_specs=[pl.BlockSpec(memory_space=pltpu.SMEM), whole, whole, whole],
        out_specs=whole,
        out_shape=jax.ShapeDtypeStruct((S, bem.shape[0]), jnp.float32),
        scratch_shapes=[pltpu.VMEM((bem.shape[1], LANES), jnp.float32)] + [square] * 4,
        compiler_params=pltpu.CompilerParams(vmem_limit_bytes=VMEM_BYTES),
        name="surface",
    )(index, values, incident, bem)


def shards(
    field, incident, elem_mat, connect, halo_lists, bem_rows, send_node, send_count, block_slots
):
    halo = halo_lists.shape[2]
    blocks = send_node.shape[1]
    slot_cap = send_node.shape[2]
    picked = pick(
        jnp.concatenate([halo_lists[0].reshape(-1), send_node[0].reshape(-1)]), field
    )
    count = lax.axis_size("row") * lax.axis_size("col")
    forward = [(i, i + 1) for i in range(count - 1)]
    backward = [(target, source) for source, target in forward]
    axes = ("row", "col")
    low = lax.ppermute(picked[:, halo : 2 * halo], axes, forward)
    high = lax.ppermute(picked[:, :halo], axes, backward)
    traces = picked[:, 2 * halo :].reshape(S, blocks, slot_cap)
    live_slots = jnp.arange(slot_cap, dtype=jnp.int32)[None, :] < send_count[0][:, None]
    traces = jnp.where(live_slots[None], traces, jnp.zeros_like(traces))
    outgoing = jnp.transpose(traces, (1, 0, 2))
    copies = lax.axis_size("row")
    spread = jnp.broadcast_to(outgoing[None], (copies,) + outgoing.shape).reshape(
        (copies * blocks,) + outgoing.shape[1:]
    )
    arrived = lax.all_to_all(spread, axes, split_axis=0, concat_axis=0, tiled=True)

    index = jnp.transpose(connect.reshape(4, -1, LANES), (1, 0, 2)).reshape(-1)
    fem_out = element_apply(index, elem_mat, low, field, high)

    values = jnp.transpose(arrived, (1, 0, 2)).reshape(S, -1)
    slots = block_slots[0].reshape(-1)
    first = jnp.sum(jnp.where(slots[None] == 0, values, 0.0), axis=1, keepdims=True)
    column = jnp.arange(incident.shape[1], dtype=jnp.int32)[None]
    incident = incident + jnp.where(column == 0, first, 0.0)
    partial_rows = surface_apply(slots, values, incident, bem_rows)
    bem_out = lax.psum(partial_rows, "col")
    return (fem_out, bem_out)


def solution(mesh):
    return jax.shard_map(
        shards,
        mesh=mesh,
        in_specs=(
            P(None, ("row", "col")),
            P(None, "col"),
            P(None, None, ("row", "col")),
            P(None, ("row", "col")),
            P(("row", "col"), None, None),
            P("row", "col"),
            P(("row", "col"), None, None),
            P(("row", "col"), None),
            P("col", None, None),
        ),
        out_specs=(P(None, ("row", "col")), P(None, "row")),
        check_vma=False,
    )
```

time: 1740 us -> 479 us (0.28)
  other arithmetic: 968 us -> 2.61 us
  local copies, waits for them, and re-layouts: 712 us -> 11.1 us
  Pallas kernels: 0 us -> 364 us
  waiting for transfers between devices: 0.01 us -> 63.8 us
    scatter-add x2 -> x0, other arithmetic: 931 us -> none  [the longest x1 782 us: element_apply(): result.at[:, target.reshape(-1)]]
    gather x4 -> x0, local copies, waits for them, and re-layouts: 618 us -> none  [the longest x2 582 us: element_apply(): gathered = extended[:, conn]]
    pallas_call x0 -> x3, Pallas kernels: none -> 364 us  [the longest x1 313 us: element_apply(): pl.pallas_call(functools.partial(element_kernel, halo), grid=(elements //...]
    ppermute x2, waiting for transfers between devices: 0.01 us -> 63.8 us  [the longest x1 63.8 us: shards(): low = lax.ppermute(picked[:, halo:2 * halo], axes, forward)]
    reshape x2 -> x0, local copies, waits for them, and re-layouts: 46 us -> none  [element_apply(): element_terms.reshape(extended.shape[0], -1)]
  transfers between devices with their start and end apart: 3 -> 3, of which waited for: 0 -> 1; matrix products, arithmetic and copies ran while one was open for 86% -> 1% of each run, Pallas kernels for 0% -> 65%
where the time goes in v1:
time: 479 us
  Pallas kernels  364 us (76%)
  waiting for transfers between devices  63.8 us (13%)
  blocking collectives  23.5 us (5%)
  starting transfers between devices  13.3 us (3%)
  local copies, waits for them, and re-layouts  11.1 us (2%)
    pallas_call x1, Pallas kernels, element_apply(): pl.pallas_call(functools.partial(element_kernel, halo), grid=(elements //...  313 us
    ppermute x1, waiting for transfers between devices, shards(): low = lax.ppermute(picked[:, halo:2 * halo], axes, forward)  63.8 us
    pallas_call x1, Pallas kernels, surface_apply(): pl.pallas_call(surface_kernel, in_specs=[pl.BlockSpec(memory_space=pltpu....  34.3 us
    psum x1, blocking collectives, shards(): bem_out = lax.psum(partial_rows, 'col')  23.5 us
    pallas_call x1, Pallas kernels, pick(): pl.pallas_call(pick_kernel, in_specs=[pl.BlockSpec(memory_space=pltpu.SME...  16.3 us
  transfers between devices with their start and end apart: 3, of which 1 were waited for; matrix products, arithmetic and copies ran while one was open for 1% of the time, Pallas kernels for 65%

profile of v1, /device:TPU:16, one launch (start us, length us, event | category | flops | bytes accessed | tf_op | source)
XLA Modules:
  0.0 478.9 jit_solution(7038312357997894462)
XLA Ops:
  0.6 0.7 reshape_squeeze.10
  1.4 0.7 reshape_squeeze.9
  2.1 0.6 pad_add_fusion.index
  2.7 16.3 %pick.1 = f32[32,9216]{1,0:T(8,128)} custom-call(s32[9216]{0:T(1024)} %pad_add_fusion.index, f32[32,6144]{1,0:T(8,128)} %field.3), custom_call_target="tpu_custom_call" | custom-call | tf_op jit(solution)/shard_map/pick/pallas_call | solution.py:69
  19.0 0.0 slice-start
  19.0 0.0 copy-start.3
  19.0 1.1 slice-done
  20.1 0.2 copy.16
  20.4 0.0 copy-done.3
  20.4 0.1 iota_compare_fusion.1
  20.5 0.1 bitcast_select_fusion.1
  20.5 0.3 copy.13
  20.8 2.0 broadcast_in_dim.55
  22.8 0.0 copy-start.1
  22.8 5.9 %all-to-all-start = ((f32[32,32,768]{2,1,0:T(8,128)}), f32[32,32,768]{2,1,0:T(8,128)S(1)}, u32[]{:S(2)}, u32[]{:S(2)}) async-start(f32[32,32,768]{2,1,0:T(8,128)} %bitcast.20), calls=%async_computation | async-start | bytes 6291456 | tf_op jit(solution)/shard_map/all_to_all | solution.py:258
  28.8 1.8 fusion.1
  30.6 2.0 collective-permute-start
  32.6 5.3 %collective-permute-start.1 = (f32[32,1536]{1,0:T(8,128)}, f32[32,1536]{1,0:T(8,128)}, u32[]{:S(2)}, u32[]{:S(2)}) collective-permute-start(f32[32,1536]{1,0:T(8,128)} %get-tuple-element.2), channel_id=1, source_target_pairs={{1,0},{2,1},{3,2},{4,3},{5,4},{6,5},{7,6},{8,7},{9,8},{10,9},{11,1... | collective-permute-start | bytes 589832 | tf_op jit(solution)/shard_map/ppermute | solution.py:249
  37.9 0.0 copy-done.1
  37.9 0.6 reshape_squeeze.11.index
  38.6 63.8 %collective-permute-done.low = f32[32,1536]{1,0:T(8,128)S(1)} collective-permute-done((f32[32,1536]{1,0:T(8,128)}, f32[32,1536]{1,0:T(8,128)S(1)}, u32[]{:S(2)}, u32[]{:S(2)}) %collective-permute-start) | collective-permute-done | bytes 196640 | tf_op jit(solution)/shard_map/ppermute | solution.py:248
  102.4 0.0 copy-start.2
  102.4 0.0 collective-permute-done.1.high
  102.4 0.7 copy-done.2
  103.0 313.4 %elements.1 = f32[32,6144]{1,0:T(8,128)} custom-call(s32[147456]{0:T(1024)} %bitcast.24, f32[4,4,36864]{2,1,0:T(4,128)} %mats.1, f32[32,1536]{1,0:T(8,128)} %copy-done.2, f32[32,6144]{1,0:T(8,128)} %field.3, f32[32,1536]{1,0:T(8,128)} %collective-permute-done.1.high), custom_call_target="tpu_custom_call" | custom-call | tf_op jit(solution)/shard_map/elements/pallas_call | solution.py:159
  416.4 0.0 all-to-all-done
  416.4 1.9 copy.15
  418.4 0.5 fusion
  418.9 0.9 copy-done
  419.8 1.4 select_add_fusion.incident
  421.1 34.3 %surface.1 = f32[32,64]{1,0:T(8,128)} custom-call(s32[24576]{0:T(1024)} %reshape_squeeze.11.index, f32[32,24576]{1,0:T(8,128)} %bitcast.21, f32[32,12288]{1,0:T(8,128)} %select_add_fusion.incident, f32[64,12288]{1,0:T(8,128)} %bem.1), custom_call_target="tpu_custom_call" | custom-call | tf_op jit(solution)/shard_map/surface/pallas_call | solution.py:224
  455.4 23.5 %psum.7 = f32[32,64]{1,0:T(8,128)} all-reduce(f32[32,64]{1,0:T(8,128)} %surface.1), channel_id=1, replica_groups=mesh['row'=4,'col'=8] {'col'}, use_global_device_ids=true, to_apply=%region_1.2 | all-reduce | flops 2048 | bytes 16384 | tf_op jit(solution)/shard_map/psum | solution.py:269
  (3 shorter events, 0.0 us)
Async XLA Ops:
  19.0 1.1 slice-start
  19.0 1.4 copy-start.3
  22.8 15.1 %copy-start.1 = (s32[1,32,768]{2,1,0:T(8,128)S(1)}, s32[1,32,768]{2,1,0:T(8,128)}, u32[]{:S(2)}) copy-start(s32[1,32,768]{2,1,0:T(8,128)} %param.17) | copy-start | bytes 294916
  22.8 393.6 %all-to-all-start = ((f32[32,32,768]{2,1,0:T(8,128)}), f32[32,32,768]{2,1,0:T(8,128)S(1)}, u32[]{:S(2)}, u32[]{:S(2)}) async-start(f32[32,32,768]{2,1,0:T(8,128)} %bitcast.20), calls=%async_computation | async-start | bytes 6291456 | tf_op jit(solution)/shard_map/all_to_all | solution.py:258
  30.6 71.8 %collective-permute-start = (f32[32,1536]{1,0:T(8,128)}, f32[32,1536]{1,0:T(8,128)S(1)}, u32[]{:S(2)}, u32[]{:S(2)}) collective-permute-start(f32[32,1536]{1,0:T(8,128)} %get-tuple-element.3), channel_id=1, source_target_pairs={{0,1},{1,2},{2,3},{3,4},{4,5},{5,6},{6,7},{7,8},{8,9},{9,10},{10,1... | collective-permute-start | bytes 589832 | tf_op jit(solution)/shard_map/ppermute | solution.py:248
  32.6 69.8 %collective-permute-start.1 = (f32[32,1536]{1,0:T(8,128)}, f32[32,1536]{1,0:T(8,128)}, u32[]{:S(2)}, u32[]{:S(2)}) collective-permute-start(f32[32,1536]{1,0:T(8,128)} %get-tuple-element.2), channel_id=1, source_target_pairs={{1,0},{2,1},{3,2},{4,3},{5,4},{6,5},{7,6},{8,7},{9,8},{10,9},{11,1... | collective-permute-start | bytes 589832 | tf_op jit(solution)/shard_map/ppermute | solution.py:249
  102.4 0.7 copy-start.2
  418.4 1.4 copy-start

commit v2 on v1

--- a/solution.py
+++ b/solution.py
@@ -83,7 +83,8 @@
     )(index, field)
 
 
-def element_kernel(halo, index, mats, low, field, high, out, table, rows, terms, *sums):
+def element_kernel(halo, index, mats, low, field, high, out, table, *scratch):
+    rows, terms, sums = scratch[:2], scratch[2:4], scratch[4:]
     step = pl.program_id(0)
     nodes = field.shape[1]
 
@@ -100,10 +101,25 @@
 
         lax.fori_loop(0, table.shape[0] // LANES, clear, 0)
 
-    def block(k, carry):
-        base = k * GROUP
-        gather_rows(table, index, base, rows)
-        turned = rows[...].T
+    count = mats.shape[2] // LANES
+
+    def gather_one(base, into, e):
+        picked = [table[pl.ds(index[base + b * LANES + e], 1), :] for b in range(4)]
+        into[pl.ds(e, 1), :] = quarter(picked)
+
+    def scatter_some(base, source, e):
+        places, values = [], []
+        for p in range(SETS):
+            term = source[pl.ds(e + p, 1), :]
+            for a in range(4):
+                place = pl.ds(index[base + a * LANES + e + p], 1)
+                places.append(place)
+                values.append(sums[4 * p + a][place, :] + term)
+        for total, place, value in zip(sums, places, values):
+            total[place, :] = value
+
+    def multiply(k, source, into):
+        turned = source[...].T
         here = aligned(k * LANES)
         parts = []
         for a in range(4):
@@ -111,26 +127,32 @@
             for b in range(1, 4):
                 part = part + mats[a, b : b + 1, here] * turned[S * b : S * b + S]
             parts.append(part)
-        terms[...] = jnp.concatenate(parts, axis=0).T
-
-        def scatter(j, inner):
-            start = pl.multiple_of(j * UNROLL, UNROLL)
-            for u in range(0, UNROLL, SETS):
-                places, values = [], []
+        into[...] = jnp.concatenate(parts, axis=0).T
+
+    gather_rows(table, index, 0, rows[0])
+    terms[1][...] = jnp.zeros((LANES, LANES), jnp.float32)
+
+    def pair(i, carry):
+        for half in range(2):
+            k = 2 * i + half
+            ahead = jnp.minimum(k + 1, count - 1) * GROUP
+            behind = jnp.maximum(k - 1, 0) * GROUP
+            multiply(k, rows[half], terms[half])
+            for e in range(0, LANES, SETS):
                 for p in range(SETS):
-                    term = terms[pl.ds(start + u + p, 1), :]
-                    for a in range(4):
-                        place = pl.ds(index[base + a * LANES + start + u + p], 1)
-                        places.append(place)
-                        values.append(sums[4 * p + a][place, :] + term)
-                for total, place, value in zip(sums, places, values):
-                    total[place, :] = value
-            return inner
-
-        lax.fori_loop(0, LANES // UNROLL, scatter, 0)
-        return carry
-
-    lax.fori_loop(0, mats.shape[2] // LANES, block, 0)
+                    gather_one(ahead, rows[1 - half], e + p)
+                scatter_some(behind, terms[1 - half], e)
+        return carry
+
+    lax.fori_loop(0, count // 2, pair, 0)
+
+    def drain(j, carry):
+        start = pl.multiple_of(j * UNROLL, UNROLL)
+        for u in range(0, UNROLL, SETS):
+            scatter_some((count - 1) * GROUP, terms[1], start + u)
+        return carry
+
+    lax.fori_loop(0, LANES // UNROLL, drain, 0)
 
     @pl.when(step == pl.num_programs(0) - 1)
     def _():
@@ -152,7 +174,7 @@
 def element_apply(index, mats, low, field, high):
     halo, nodes = low.shape[1], field.shape[1]
     elements = mats.shape[2]
-    blocks = next(n for n in (16, 12, 8, 4, 2) if elements % (n * LANES) == 0)
+    blocks = next(n for n in (48, 32, 24, 16, 12, 8, 4, 2) if elements % (n * LANES) == 0)
     table = pltpu.VMEM((nodes + 2 * halo, LANES), jnp.float32)
     square = pltpu.VMEM((LANES, LANES), jnp.float32)
     whole = pl.BlockSpec(memory_space=pltpu.VMEM)
@@ -168,7 +190,7 @@
         ],
         out_specs=whole,
         out_shape=jax.ShapeDtypeStruct((S, nodes), jnp.float32),
-        scratch_shapes=[table, square, square] + [table] * (4 * SETS),
+        scratch_shapes=[table] + [square] * 4 + [table] * (4 * SETS),
         compiler_params=pltpu.CompilerParams(vmem_limit_bytes=VMEM_BYTES),
         name="elements",
     )(index, mats, low, field, high)

time: 479 us -> 425 us (0.89)
  Pallas kernels: 364 us -> 309 us
    pallas_call x1, Pallas kernels: 313 us -> 259 us  [element_apply(): pl.pallas_call(functools.partial(element_kernel, halo), grid=(elements //...]
  transfers between devices with their start and end apart: 3 -> 3, of which waited for: 1 -> 1; matrix products, arithmetic and copies ran while one was open for 1% -> 1% of each run, Pallas kernels for 65% -> 61%
where the time goes in v2:
time: 425 us; the launch traced here: 424 us
  Pallas kernels  309 us (73%)
  waiting for transfers between devices  63.8 us (15%)
  blocking collectives  23.5 us (6%)
  starting transfers between devices  13.3 us (3%)
  local copies, waits for them, and re-layouts  11.1 us (3%)
    pallas_call x1, Pallas kernels, element_apply(): pl.pallas_call(functools.partial(element_kernel, halo), grid=(elements //...  259 us
    ppermute x1, waiting for transfers between devices, shards(): low = lax.ppermute(picked[:, halo:2 * halo], axes, forward)  63.8 us
    pallas_call x1, Pallas kernels, surface_apply(): pl.pallas_call(surface_kernel, in_specs=[pl.BlockSpec(memory_space=pltpu....  34.3 us
    psum x1, blocking collectives, shards(): bem_out = lax.psum(partial_rows, 'col')  23.5 us
    pallas_call x1, Pallas kernels, pick(): pl.pallas_call(pick_kernel, in_specs=[pl.BlockSpec(memory_space=pltpu.SME...  16.3 us
  transfers between devices with their start and end apart: 3, of which 1 were waited for; matrix products, arithmetic and copies ran while one was open for 1% of the time, Pallas kernels for 61%

profile of v2, /device:TPU:16, one launch (start us, length us, event | category | flops | bytes accessed | tf_op | source)
XLA Modules:
  0.0 424.2 jit_solution(16327650315840085703)
XLA Ops:
  0.6 0.7 reshape_squeeze.10
  1.4 0.7 reshape_squeeze.9
  2.1 0.6 pad_add_fusion.index
  2.7 16.3 %pick.1 = f32[32,9216]{1,0:T(8,128)} custom-call(s32[9216]{0:T(1024)} %pad_add_fusion.index, f32[32,6144]{1,0:T(8,128)} %field.3), custom_call_target="tpu_custom_call" | custom-call | tf_op jit(solution)/shard_map/pick/pallas_call | solution.py:69
  19.0 0.0 slice-start
  19.0 0.0 copy-start.3
  19.0 1.1 slice-done
  20.1 0.2 copy.16
  20.4 0.0 copy-done.3
  20.4 0.1 iota_compare_fusion.1
  20.5 0.1 bitcast_select_fusion.1
  20.5 0.3 copy.13
  20.8 2.0 broadcast_in_dim.55
  22.8 0.0 copy-start.1
  22.8 5.9 %all-to-all-start = ((f32[32,32,768]{2,1,0:T(8,128)}), f32[32,32,768]{2,1,0:T(8,128)S(1)}, u32[]{:S(2)}, u32[]{:S(2)}) async-start(f32[32,32,768]{2,1,0:T(8,128)} %bitcast.20), calls=%async_computation | async-start | bytes 6291456 | tf_op jit(solution)/shard_map/all_to_all | solution.py:280
  28.8 1.8 fusion.1
  30.6 2.0 collective-permute-start
  32.6 5.3 %collective-permute-start.1 = (f32[32,1536]{1,0:T(8,128)}, f32[32,1536]{1,0:T(8,128)}, u32[]{:S(2)}, u32[]{:S(2)}) collective-permute-start(f32[32,1536]{1,0:T(8,128)} %get-tuple-element.2), channel_id=1, source_target_pairs={{1,0},{2,1},{3,2},{4,3},{5,4},{6,5},{7,6},{8,7},{9,8},{10,9},{11,1... | collective-permute-start | bytes 589832 | tf_op jit(solution)/shard_map/ppermute | solution.py:271
  37.9 0.0 copy-done.1
  37.9 0.6 reshape_squeeze.11.index
  38.6 63.8 %collective-permute-done.low = f32[32,1536]{1,0:T(8,128)S(1)} collective-permute-done((f32[32,1536]{1,0:T(8,128)}, f32[32,1536]{1,0:T(8,128)S(1)}, u32[]{:S(2)}, u32[]{:S(2)}) %collective-permute-start) | collective-permute-done | bytes 196640 | tf_op jit(solution)/shard_map/ppermute | solution.py:270
  102.4 0.0 copy-start.2
  102.4 0.0 collective-permute-done.1.high
  102.4 0.7 copy-done.2
  103.0 258.6 %elements.1 = f32[32,6144]{1,0:T(8,128)} custom-call(s32[147456]{0:T(1024)} %bitcast.24, f32[4,4,36864]{2,1,0:T(4,128)} %mats.1, f32[32,1536]{1,0:T(8,128)} %copy-done.2, f32[32,6144]{1,0:T(8,128)} %field.3, f32[32,1536]{1,0:T(8,128)} %collective-permute-done.1.high), custom_call_target="tpu_custom_call" | custom-call | tf_op jit(solution)/shard_map/elements/pallas_call | solution.py:181
  361.6 0.0 all-to-all-done
  361.7 1.9 copy.15
  363.6 0.5 fusion
  364.1 0.9 copy-done
  365.0 1.4 select_add_fusion.incident
  366.4 34.3 %surface.1 = f32[32,64]{1,0:T(8,128)} custom-call(s32[24576]{0:T(1024)} %reshape_squeeze.11.index, f32[32,24576]{1,0:T(8,128)} %bitcast.21, f32[32,12288]{1,0:T(8,128)} %select_add_fusion.incident, f32[64,12288]{1,0:T(8,128)} %bem.1), custom_call_target="tpu_custom_call" | custom-call | tf_op jit(solution)/shard_map/surface/pallas_call | solution.py:246
  400.7 23.5 %psum.7 = f32[32,64]{1,0:T(8,128)} all-reduce(f32[32,64]{1,0:T(8,128)} %surface.1), channel_id=1, replica_groups=mesh['row'=4,'col'=8] {'col'}, use_global_device_ids=true, to_apply=%region_1.2 | all-reduce | flops 2048 | bytes 16384 | tf_op jit(solution)/shard_map/psum | solution.py:291
  (3 shorter events, 0.0 us)
Async XLA Ops:
  19.0 1.1 slice-start
  19.0 1.4 copy-start.3
  22.8 15.1 %copy-start.1 = (s32[1,32,768]{2,1,0:T(8,128)S(1)}, s32[1,32,768]{2,1,0:T(8,128)}, u32[]{:S(2)}) copy-start(s32[1,32,768]{2,1,0:T(8,128)} %param.17) | copy-start | bytes 294916
  22.8 338.8 %all-to-all-start = ((f32[32,32,768]{2,1,0:T(8,128)}), f32[32,32,768]{2,1,0:T(8,128)S(1)}, u32[]{:S(2)}, u32[]{:S(2)}) async-start(f32[32,32,768]{2,1,0:T(8,128)} %bitcast.20), calls=%async_computation | async-start | bytes 6291456 | tf_op jit(solution)/shard_map/all_to_all | solution.py:280
  30.6 71.8 %collective-permute-start = (f32[32,1536]{1,0:T(8,128)}, f32[32,1536]{1,0:T(8,128)S(1)}, u32[]{:S(2)}, u32[]{:S(2)}) collective-permute-start(f32[32,1536]{1,0:T(8,128)} %get-tuple-element.3), channel_id=1, source_target_pairs={{0,1},{1,2},{2,3},{3,4},{4,5},{5,6},{6,7},{7,8},{8,9},{9,10},{10,1... | collective-permute-start | bytes 589832 | tf_op jit(solution)/shard_map/ppermute | solution.py:270
  32.6 69.8 %collective-permute-start.1 = (f32[32,1536]{1,0:T(8,128)}, f32[32,1536]{1,0:T(8,128)}, u32[]{:S(2)}, u32[]{:S(2)}) collective-permute-start(f32[32,1536]{1,0:T(8,128)} %get-tuple-element.2), channel_id=1, source_target_pairs={{1,0},{2,1},{3,2},{4,3},{5,4},{6,5},{7,6},{8,7},{9,8},{10,9},{11,1... | collective-permute-start | bytes 589832 | tf_op jit(solution)/shard_map/ppermute | solution.py:271
  102.4 0.7 copy-start.2
  363.6 1.4 copy-start
